TPU v7x, 256 devices: a whole 4x4x8 slice. The times are simulated.
256 devices in a mesh: region: 32 (over x, z), band: 8 (over y, core).
Axes of the slice: x: 4, y: 4, z: 8, core: 2. Of those that a mesh axis runs over, the one named last changes fastest.
Arguments:
- probes: bfloat16 [4, 4, 1024, 32768], P(None, None, 'band', 'region'), may hold values from -5 to 5
- filter_taps: float32 [2, 2, 17], replicated, may hold values from 0.02 to 1
- mixing: float32 [2, 4, 4], replicated, as said below
- nugget: float32 [4], replicated, may hold values from 0.3 to 1.5
- land_span: int32 [2, 1024, 32], P(None, 'band', 'region'), may hold values from 0 to 1024, as said below
Outputs:
- covariance_probes: bfloat16 [4, 4, 1024, 32768], P(None, None, 'band', 'region')
- quadratic: float32 [4, 3], replicated
Inputs may be any that keep to these rules, and one draw needn't show every extreme that they name: Row r of region block b has land in the columns land_span[0, r, b] to land_span[1, r, b] - 1 of the block; land_span[0] <= land_span[1] everywhere. `mixing`: each of the 2 matrices is symmetric positive definite.
All inputs are finite; a program needn't handle non-finite values.
Results may differ from a plain program's by a relative error of at most 0.0062.
Values may be sent and summed in bfloat16 or wider, within the bound.
A program may use at most 128 MiB of HBM per device.

v0:
```python
import functools

import jax
import jax.numpy as jnp
from jax import lax
from jax.experimental import pallas as pl
from jax.experimental.pallas import tpu as pltpu
from jax.sharding import PartitionSpec as P

MESH = pl.DeviceIdType.MESH
BF16 = jnp.bfloat16
F32 = jnp.float32

PROBES, VARS, KERNELS, HALF = 4, 4, 2, 16
PLANES = PROBES * VARS
LANES = 128
TILE = 32
WINDOW = TILE + 2 * HALF
GROUP = LANES // HALF


def toeplitz(distance, tap):
    reach = jnp.abs(distance - HALF)
    total = jnp.zeros(distance.shape, F32)
    for step in range(HALF + 1):
        total = jnp.where(reach == step, tap(step), total)
    return total


def lane_of(rows):
    return lax.broadcasted_iota(jnp.int32, (rows, LANES), 1)


def kernel(
    probes, taps, mixing, nugget, span, out, quad,
    held, land, padded, across, staged, column_filter, row_filter, edges,
    row_halo, col_halo, corner_halo, partial, shares, slots_a, slots_b, slots_c,
    load_sem, row_send, row_recv, col_send, col_recv, corner_send, corner_recv,
    store_sem, share_send, share_recv,
):
    rows, cols = held.shape[1:]
    blocks = cols // LANES
    regions, bands = lax.axis_size("region"), lax.axis_size("band")
    across_z = 8 if regions % 8 == 0 else regions
    across_x = regions // across_z
    region, band = lax.axis_index("region"), lax.axis_index("band")
    east, west = lax.rem(region + 1, regions), lax.rem(region + regions - 1, regions)
    south, north = lax.rem(band + 1, bands), lax.rem(band + bands - 1, bands)
    base_z = lax.div(region, across_z) * across_z
    at_z = lax.rem(region, across_z)

    band_peers = [(region, lax.rem(band + d, bands)) for d in range(1, bands)]
    z_peers = [(base_z + lax.rem(at_z + d, across_z), band) for d in range(1, across_z)]
    x_peers = [(lax.rem(region + d * across_z, regions), band) for d in range(1, across_x)]
    corners = [(east, south), (east, north), (west, south), (west, north)]
    greeted = band_peers + z_peers + x_peers + [(east, band), (west, band)] + corners

    loads = [
        pltpu.make_async_copy(
            probes.at[pl.ds(VARS * p, VARS)], held.at[pl.ds(VARS * p, VARS)], load_sem.at[p]
        )
        for p in range(PROBES)
    ]
    for load in loads:
        load.start()
    barrier = pltpu.get_barrier_semaphore()
    for peer in greeted:
        pl.semaphore_signal(barrier, inc=1, device_id=peer, device_id_type=MESH)

    def by_row(entry):
        line = span[entry].astype(F32)
        return jnp.transpose(jnp.broadcast_to(line, (LANES, rows)))

    lower, upper = by_row(0), by_row(1)
    for block in range(blocks):
        column = (lane_of(rows) + block * LANES).astype(F32)
        inside = (column >= lower) & (column < upper)
        land[:, block * LANES : (block + 1) * LANES] = jnp.where(inside, 1.0, 0.0).astype(BF16)

    def rounded(k, axis):
        return lambda step: jnp.full((1, 1), taps[k, axis, step], F32).astype(BF16).astype(F32)

    shape = (2 * LANES, LANES)
    offset = lax.broadcasted_iota(jnp.int32, shape, 0) - lax.broadcasted_iota(jnp.int32, shape, 1)
    for k in range(KERNELS):
        column_filter[:, k * LANES : (k + 1) * LANES] = toeplitz(offset, rounded(k, 0)).astype(BF16)
    shape = (TILE, LANES)
    lane = lax.broadcasted_iota(jnp.int32, shape, 1)
    offset = lax.rem(lane, WINDOW) - lax.broadcasted_iota(jnp.int32, shape, 0)
    for k in range(KERNELS):
        pattern = toeplitz(offset, rounded(k, 1))
        for v in range(VARS):
            for w in range(0, VARS, 2):
                gains = jnp.where(lane < WINDOW, mixing[k, v, w], mixing[k, v, w + 1])
                row_filter[k, v * TILE : (v + 1) * TILE, w * WINDOW : (w + 2) * WINDOW] = (
                    gains * pattern
                ).astype(BF16)

    lanes = lane_of(rows)
    zero = jnp.zeros((rows, LANES), BF16)

    def shifted(block, first, store):
        previous = first
        for j in range(blocks):
            current = pltpu.roll(block(j), HALF, 1)
            store(j, jnp.where(lane_of(current.shape[0]) < HALF, previous, current))
            previous = current
        return previous

    def mask_planes(p):
        loads[p].wait()
        for v in range(VARS):
            q = VARS * p + v
            held[q] = held[q] * land[...]

    def row_copies(p):
        some = pl.ds(VARS * p, VARS)
        return [
            pltpu.make_async_remote_copy(
                held.at[some, pl.ds(rows - HALF, HALF)], row_halo.at[0, some],
                row_send.at[0, p], row_recv.at[0, p], device_id=(region, south),
                device_id_type=MESH,
            ),
            pltpu.make_async_remote_copy(
                held.at[some, pl.ds(0, HALF)], row_halo.at[1, some],
                row_send.at[1, p], row_recv.at[1, p], device_id=(region, north),
                device_id_type=MESH,
            ),
        ]

    def edge_copies(g):
        copies = []
        for side, target in ((0, west), (1, east)):
            copies.append(
                pltpu.make_async_remote_copy(
                    edges.at[side, g], col_halo.at[1 - side, g],
                    col_send.at[side, g], col_recv.at[1 - side, g],
                    device_id=(target, band), device_id_type=MESH,
                )
            )
        for side, target in ((0, west), (1, east)):
            for end, line in ((0, north), (1, south)):
                copies.append(
                    pltpu.make_async_remote_copy(
                        edges.at[side, g, pl.ds(end * (rows - HALF), HALF)],
                        corner_halo.at[1 - side, 1 - end, g],
                        corner_send.at[side, end, g], corner_recv.at[1 - side, 1 - end, g],
                        device_id=(target, line), device_id_type=MESH,
                    )
                )
        return copies

    def pack_edges(g):
        west_edge, east_edge = zero, zero
        for a in range(GROUP):
            q = GROUP * g + a
            both = jnp.where(lanes < HALF, held[q, :, :LANES], held[q, :, cols - LANES :])
            both = pltpu.roll(both, a * HALF, 1) if a else both
            slot = lax.div(lanes, HALF)
            west_edge = jnp.where(slot == a, both, west_edge)
            east_edge = jnp.where(slot == (a - 1) % GROUP, both, east_edge)
        edges[0, g] = west_edge
        edges[1, g] = east_edge

    row_moves, edge_moves = [], []
    for p in range(PROBES):
        mask_planes(p)
        if p == 0:
            pl.semaphore_wait(barrier, len(greeted))
        row_moves.append(row_copies(p))
        for move in row_moves[-1]:
            move.start()
        if (p + 1) * VARS % GROUP == 0:
            g = p * VARS // GROUP
            pack_edges(g)
            edge_moves.append(edge_copies(g))
            for move in edge_moves[-1]:
                move.start()

    def shift_planes(number, carry):
        for u in range(4):
            q = 4 * number + u

            def store(j, value):
                padded[q, HALF : HALF + rows, j * LANES : (j + 1) * LANES] = value

            last = shifted(lambda j: held[q, :, j * LANES : (j + 1) * LANES], zero, store)
            store(blocks, jnp.where(lanes < HALF, last, zero))
        return carry

    lax.fori_loop(0, PLANES // 4, shift_planes, 0)

    def filter_columns(number, carry, chosen):
        for u in range(4):
            q = 4 * number + u
            for j in chosen:
                window = padded[q, HALF : HALF + rows, j * LANES : (j + 2) * LANES]
                both = jnp.dot(
                    window, column_filter[...], preferred_element_type=F32
                ).astype(BF16)
                for k in range(KERNELS):
                    across[k, q, HALF : HALF + rows, j * LANES : (j + 1) * LANES] = both[
                        :, k * LANES : (k + 1) * LANES
                    ]
        return carry

    lax.fori_loop(
        0, PLANES // 4, functools.partial(filter_columns, chosen=range(1, blocks - 1)), 0
    )

    def unpack(west_halo, east_halo, a):
        slot = lax.div(lane_of(west_halo.shape[0]), HALF)
        both = jnp.where(slot == a, east_halo, west_halo)
        turn = (LANES - (a - 1) * HALF) % LANES
        return pltpu.roll(both, turn, 1) if turn else both

    for g in range(PLANES // GROUP):
        for move in edge_moves[g][:2]:
            move.wait_recv()
        for a in range(GROUP):
            q = GROUP * g + a
            halo = unpack(col_halo[0, g], col_halo[1, g], a)
            own = pl.ds(HALF, rows)
            padded[q, own, :LANES] = jnp.where(lanes < HALF, halo, padded[q, own, :LANES])
            tail = jnp.where(lanes < 2 * HALF, halo, zero)
            padded[q, own, cols:] = jnp.where(lanes < HALF, padded[q, own, cols:], tail)
    lax.fori_loop(0, PLANES // 4, functools.partial(filter_columns, chosen=(0, blocks - 1)), 0)

    width = 2 * LANES
    partial[...] = jnp.zeros_like(partial)

    def folded(value):
        value = jnp.sum(value.reshape(-1, 8, width), axis=0)
        return value[:, :LANES] + value[:, LANES:]

    def finish_tiles(p, tiles):
        first = VARS * p
        for tile in tiles:
            own = pl.ds(tile * TILE, TILE)
            for chunk in range(cols // width):
                part = pl.ds(chunk * width, width)
                terms = []
                for k in range(KERNELS):
                    stack = jnp.concatenate(
                        [
                            across[k, first + w, pl.ds(tile * TILE, WINDOW), part]
                            for w in range(VARS)
                        ],
                        axis=0,
                    )
                    terms.append(jnp.dot(row_filter[k], stack, preferred_element_type=F32))
                keep = land[own, part] != 0
                sums = [jnp.zeros((8, LANES), F32) for _ in range(KERNELS + 1)]
                for v in range(VARS):
                    local = held[first + v, own, part].astype(F32)
                    noise = nugget[v] * local
                    mixed = [term[v * TILE : (v + 1) * TILE] for term in terms]
                    total = (mixed[0] + mixed[1] + noise).astype(BF16)
                    staged[first + v, own, part] = jnp.where(keep, total, jnp.zeros_like(total))
                    for k, term in enumerate(mixed + [noise]):
                        sums[k] = sums[k] + folded(term * local)
                for k in range(KERNELS + 1):
                    partial[k, p] = partial[k, p] + sums[k]

    def inner_tiles(p, carry):
        finish_tiles(p, range(1, rows // TILE - 1))
        return carry

    lax.fori_loop(0, PROBES, inner_tiles, 0)

    for g in range(PLANES // GROUP):
        for move in edge_moves[g][2:]:
            move.wait_recv()
    for p in range(PROBES):
        for move in row_moves[p]:
            move.wait_recv()

    beyond = [(band > 0).astype(F32).astype(BF16), (band < bands - 1).astype(F32).astype(BF16)]
    short = lane_of(HALF)
    none = jnp.zeros((HALF, LANES), BF16)
    def halo_rows(g, carry):
        for a in range(GROUP):
            q = GROUP * g + a
            for end, place in ((0, 0), (1, HALF + rows)):
                halo = unpack(corner_halo[0, end, g], corner_halo[1, end, g], a)

                def store(j, value):
                    padded[q, place : place + HALF, j * LANES : (j + 1) * LANES] = (
                        value * beyond[end]
                    )

                last = shifted(
                    lambda j: row_halo[end, q, :, j * LANES : (j + 1) * LANES], halo, store
                )
                tail = jnp.where(short < 2 * HALF, halo, none)
                store(blocks, jnp.where(short < HALF, last, tail))
        return carry

    lax.fori_loop(0, PLANES // GROUP, halo_rows, 0)

    def filter_halo(number, carry):
        ends = (0, HALF + rows)
        for j in range(blocks):
            part = slice(j * LANES, (j + 2) * LANES)
            window = jnp.concatenate(
                [padded[4 * number + u, at : at + HALF, part] for u in range(4) for at in ends],
                axis=0,
            )
            both = jnp.dot(window, column_filter[...], preferred_element_type=F32).astype(BF16)
            for u in range(4):
                for end, at in enumerate(ends):
                    start = (2 * u + end) * HALF
                    for k in range(KERNELS):
                        across[
                            k, 4 * number + u, at : at + HALF, j * LANES : (j + 1) * LANES
                        ] = both[start : start + HALF, k * LANES : (k + 1) * LANES]
        return carry

    lax.fori_loop(0, PLANES // 4, filter_halo, 0)

    def outer_tiles(p, carry):
        finish_tiles(p, (0, rows // TILE - 1))
        some = pl.ds(VARS * p, VARS)
        pltpu.make_async_copy(staged.at[some], out.at[some], store_sem.at[p]).start()
        return carry

    lax.fori_loop(0, PROBES, outer_tiles, 0)

    value = jnp.sum(partial[...].reshape(-1, 8, LANES), axis=1)
    for number, (peers, slots) in enumerate(
        ((band_peers, slots_a), (z_peers, slots_b), (x_peers, slots_c))
    ):
        if not peers:
            continue
        shares[number] = value
        moves = [
            pltpu.make_async_remote_copy(
                shares.at[number], slots.at[d], share_send.at[number, d], share_recv.at[number, d],
                device_id=peer, device_id_type=MESH,
            )
            for d, peer in enumerate(peers)
        ]
        for move in moves:
            move.start()
        for d, move in enumerate(moves):
            move.wait()
        for d in range(len(peers)):
            value = value + slots[d]
    value = jnp.sum(value, axis=1, keepdims=True) * (1.0 / (bands * rows * cols))
    for k in range(KERNELS + 1):
        quad[:, k : k + 1] = value[k * PROBES : (k + 1) * PROBES]

    for moves in row_moves + edge_moves:
        for move in moves:
            move.wait_send()
    for p in range(PROBES):
        some = pl.ds(VARS * p, VARS)
        pltpu.make_async_copy(staged.at[some], out.at[some], store_sem.at[p]).wait()


def per_device(probes, filter_taps, mixing, nugget, land_span):
    rows, cols = probes.shape[2:]
    bands = lax.axis_size("band")
    any_space = pl.BlockSpec(memory_space=pl.ANY)
    scalars = pl.BlockSpec(memory_space=pltpu.SMEM)
    vector = pl.BlockSpec(memory_space=pltpu.VMEM)
    count = (KERNELS + 1) * PROBES
    dma = pltpu.SemaphoreType.DMA
    out, quadratic = pl.pallas_call(
        kernel,
        out_shape=(
            jax.ShapeDtypeStruct((PLANES, rows, cols), BF16),
            jax.ShapeDtypeStruct((PROBES, KERNELS + 1), F32),
        ),
        in_specs=[any_space, scalars, scalars, scalars, vector],
        out_specs=(any_space, vector),
        scratch_shapes=[
            pltpu.VMEM((PLANES, rows, cols), BF16),
            pltpu.VMEM((rows, cols), BF16),
            pltpu.VMEM((PLANES, rows + 2 * HALF, cols + LANES), BF16),
            pltpu.VMEM((KERNELS, PLANES, rows + 2 * HALF, cols), BF16),
            pltpu.VMEM((PLANES, rows, cols), BF16),
            pltpu.VMEM((2 * LANES, KERNELS * LANES), BF16),
            pltpu.VMEM((KERNELS, VARS * TILE, VARS * WINDOW), BF16),
            pltpu.VMEM((2, PLANES // GROUP, rows, LANES), BF16),
            pltpu.VMEM((2, PLANES, HALF, cols), BF16),
            pltpu.VMEM((2, PLANES // GROUP, rows, LANES), BF16),
            pltpu.VMEM((2, 2, PLANES // GROUP, HALF, LANES), BF16),
            pltpu.VMEM((KERNELS + 1, PROBES, 8, LANES), F32),
            pltpu.VMEM((3, count, LANES), F32),
            pltpu.VMEM((max(bands - 1, 1), count, LANES), F32),
            pltpu.VMEM((7, count, LANES), F32),
            pltpu.VMEM((3, count, LANES), F32),
            dma((PROBES,)),
            dma((2, PROBES)),
            dma((2, PROBES)),
            dma((2, PLANES // GROUP)),
            dma((2, PLANES // GROUP)),
            dma((2, 2, PLANES // GROUP)),
            dma((2, 2, PLANES // GROUP)),
            dma((PROBES,)),
            dma((3, 7)),
            dma((3, 7)),
        ],
        compiler_params=pltpu.CompilerParams(
            collective_id=0, has_side_effects=True, vmem_limit_bytes=56 * 1024 * 1024
        ),
    )(
        probes.reshape(PLANES, rows, cols),
        filter_taps,
        mixing,
        nugget,
        jnp.transpose(land_span, (0, 2, 1)),
    )
    return out.reshape(PROBES, VARS, rows, cols), quadratic


def solution(mesh):
    return jax.shard_map(
        per_device,
        mesh=mesh,
        in_specs=(P(None, None, "band", "region"), P(), P(), P(), P(None, "band", "region")),
        out_specs=(P(None, None, "band", "region"), P()),
        check_vma=False,
    )
```

profile of v0, /device:TPU:1, one launch (start us, length us, event | category | flops | bytes accessed | tf_op | source)
XLA Modules:
  0.0 42.0 jit_solution(17326794630714289628)
XLA Ops:
  0.6 36.0 %shard_map.68 = (bf16[16,128,1024]{2,1,0:T(8,128)(2,1)}, f32[4,3]{1,0:T(4,128)}) custom-call(bf16[16,128,1024]{2,1,0:T(8,128)(2,1)} %bitcast.3, f32[2,2,17]{2,1,0:T(2,128)} %taps.1, f32[2,4,4]{2,1,0:T(4,128)} %mixing.1, f32[4]{0:T(128)} %nugget.1, s32[2,1,128]{2,1,0:T(1,128)} %bitcast.5), custom_call_target="tpu_custom_call" | custom-call | tf_op jit(solution)/shard_map/pallas_call | solution.py:369
  36.6 0.0 copy-start
  36.6 4.8 %copy.9 = bf16[4,4,128,1024]{3,2,1,0:T(8,128)(2,1)} copy(bf16[4,4,128,1024]{3,2,1,0:T(8,128)(2,1)} %bitcast.4) | data formatting | bytes 8388608
  41.4 0.0 copy-done
  41.4 0.6 %copy.10 = f32[4,3]{1,0:T(4,128)} copy(f32[4,3]{1,0:T(4,128)S(1)} %copy-done) | data formatting | bytes 96
Async XLA Ops:
  36.6 4.8 %copy-start = (f32[4,3]{1,0:T(4,128)S(1)}, f32[4,3]{1,0:T(4,128)}, u32[]{:S(2)}) copy-start(f32[4,3]{1,0:T(4,128)} %get-tuple-element.9) | copy-start | bytes 148
where the time goes:
time: 42.1 us; the launch traced here: 42 us
  Pallas kernels  36 us (86%)
  local copies, waits for them, and re-layouts  5.39 us (13%)
  between operations  0.65 us (2%)
    pallas_call x1, Pallas kernels, per_device(): pl.pallas_call(kernel, out_shape=(jax.ShapeDtypeStruct((PLANES, rows, col...  36 us
    unnamed x4, local copies, waits for them, and re-layouts  5.39 us

commit v1 on v0

--- a/solution.py
+++ b/solution.py
@@ -33,10 +33,10 @@
 
 def kernel(
     probes, taps, mixing, nugget, span, out, quad,
-    held, land, padded, across, staged, column_filter, row_filter, edges,
-    row_halo, col_halo, corner_halo, partial, shares, slots_a, slots_b, slots_c,
+    held, land, padded, across, column_filter, row_filter, edges,
+    row_halo, col_halo, corner_halo, partial, shares, slots_a, slots_b,
     load_sem, row_send, row_recv, col_send, col_recv, corner_send, corner_recv,
-    store_sem, share_send, share_recv,
+    share_send, share_recv,
 ):
     rows, cols = held.shape[1:]
     blocks = cols // LANES
@@ -49,11 +49,19 @@
     base_z = lax.div(region, across_z) * across_z
     at_z = lax.rem(region, across_z)
 
-    band_peers = [(region, lax.rem(band + d, bands)) for d in range(1, bands)]
-    z_peers = [(base_z + lax.rem(at_z + d, across_z), band) for d in range(1, across_z)]
-    x_peers = [(lax.rem(region + d * across_z, regions), band) for d in range(1, across_x)]
+    cores = 2
+    strips = bands // cores
+    at_y, core = lax.div(band, cores), lax.rem(band, cores)
+    near = [
+        (base_z + lax.rem(at_z + d // cores, across_z), at_y * cores + lax.rem(core + d, cores))
+        for d in range(1, across_z * cores)
+    ]
+    far = [
+        (lax.rem(region + d // strips * across_z, regions), lax.rem(band + d % strips * cores, bands))
+        for d in range(1, across_x * strips)
+    ]
     corners = [(east, south), (east, north), (west, south), (west, north)]
-    greeted = band_peers + z_peers + x_peers + [(east, band), (west, band)] + corners
+    greeted = near + far + [(region, south), (region, north), (east, band), (west, band)] + corners
 
     loads = [
         pltpu.make_async_copy(
@@ -98,6 +106,10 @@
 
     lanes = lane_of(rows)
     zero = jnp.zeros((rows, LANES), BF16)
+    own = slice(HALF, HALF + rows)
+
+    def columns(j, count=1):
+        return slice(j * LANES, (j + count) * LANES)
 
     def shifted(block, first, store):
         previous = first
@@ -106,12 +118,6 @@
             store(j, jnp.where(lane_of(current.shape[0]) < HALF, previous, current))
             previous = current
         return previous
-
-    def mask_planes(p):
-        loads[p].wait()
-        for v in range(VARS):
-            q = VARS * p + v
-            held[q] = held[q] * land[...]
 
     def row_copies(p):
         some = pl.ds(VARS * p, VARS)
@@ -150,21 +156,46 @@
                 )
         return copies
 
-    def pack_edges(g):
-        west_edge, east_edge = zero, zero
-        for a in range(GROUP):
-            q = GROUP * g + a
-            both = jnp.where(lanes < HALF, held[q, :, :LANES], held[q, :, cols - LANES :])
-            both = pltpu.roll(both, a * HALF, 1) if a else both
-            slot = lax.div(lanes, HALF)
-            west_edge = jnp.where(slot == a, both, west_edge)
-            east_edge = jnp.where(slot == (a - 1) % GROUP, both, east_edge)
-        edges[0, g] = west_edge
-        edges[1, g] = east_edge
+    def mask_borders(q, a, packed):
+        for place in (slice(0, HALF), slice(rows - HALF, rows)):
+            held[q, place] = held[q, place] * land[place]
+        both = jnp.where(lanes < HALF, held[q, :, columns(0)], held[q, :, columns(blocks - 1)])
+        both = both * jnp.where(lanes < HALF, land[:, columns(0)], land[:, columns(blocks - 1)])
+        both = pltpu.roll(both, a * HALF, 1) if a else both
+        slot = lax.div(lanes, HALF)
+        return [
+            jnp.where(slot == a, both, packed[0]),
+            jnp.where(slot == (a - 1) % GROUP, both, packed[1]),
+        ]
+
+    def mask_and_shift(q):
+        inner = slice(HALF, rows - HALF)
+
+        def block(j):
+            value = held[q, :, columns(j)] * land[:, columns(j)]
+            held[q, inner, columns(j)] = value[inner]
+            return value
+
+        def store(j, value):
+            padded[q, own, columns(j)] = value
+
+        last = shifted(block, zero, store)
+        store(blocks, jnp.where(lanes < HALF, last, zero))
+
+    def filter_plane(q, chosen):
+        for j in chosen:
+            both = jnp.dot(
+                padded[q, own, columns(j, 2)], column_filter[...], preferred_element_type=F32
+            ).astype(BF16)
+            for k in range(KERNELS):
+                across[k, q, own, columns(j)] = both[:, columns(k)]
 
     row_moves, edge_moves = [], []
+    packed = [zero, zero]
     for p in range(PROBES):
-        mask_planes(p)
+        loads[p].wait()
+        for q in range(VARS * p, VARS * (p + 1)):
+            packed = mask_borders(q, q % GROUP, packed)
         if p == 0:
             pl.semaphore_wait(barrier, len(greeted))
         row_moves.append(row_copies(p))
@@ -172,59 +203,14 @@
             move.start()
         if (p + 1) * VARS % GROUP == 0:
             g = p * VARS // GROUP
-            pack_edges(g)
+            edges[0, g], edges[1, g] = packed
+            packed = [zero, zero]
             edge_moves.append(edge_copies(g))
             for move in edge_moves[-1]:
                 move.start()
-
-    def shift_planes(number, carry):
-        for u in range(4):
-            q = 4 * number + u
-
-            def store(j, value):
-                padded[q, HALF : HALF + rows, j * LANES : (j + 1) * LANES] = value
-
-            last = shifted(lambda j: held[q, :, j * LANES : (j + 1) * LANES], zero, store)
-            store(blocks, jnp.where(lanes < HALF, last, zero))
-        return carry
-
-    lax.fori_loop(0, PLANES // 4, shift_planes, 0)
-
-    def filter_columns(number, carry, chosen):
-        for u in range(4):
-            q = 4 * number + u
-            for j in chosen:
-                window = padded[q, HALF : HALF + rows, j * LANES : (j + 2) * LANES]
-                both = jnp.dot(
-                    window, column_filter[...], preferred_element_type=F32
-                ).astype(BF16)
-                for k in range(KERNELS):
-                    across[k, q, HALF : HALF + rows, j * LANES : (j + 1) * LANES] = both[
-                        :, k * LANES : (k + 1) * LANES
-                    ]
-        return carry
-
-    lax.fori_loop(
-        0, PLANES // 4, functools.partial(filter_columns, chosen=range(1, blocks - 1)), 0
-    )
-
-    def unpack(west_halo, east_halo, a):
-        slot = lax.div(lane_of(west_halo.shape[0]), HALF)
-        both = jnp.where(slot == a, east_halo, west_halo)
-        turn = (LANES - (a - 1) * HALF) % LANES
-        return pltpu.roll(both, turn, 1) if turn else both
-
-    for g in range(PLANES // GROUP):
-        for move in edge_moves[g][:2]:
-            move.wait_recv()
-        for a in range(GROUP):
-            q = GROUP * g + a
-            halo = unpack(col_halo[0, g], col_halo[1, g], a)
-            own = pl.ds(HALF, rows)
-            padded[q, own, :LANES] = jnp.where(lanes < HALF, halo, padded[q, own, :LANES])
-            tail = jnp.where(lanes < 2 * HALF, halo, zero)
-            padded[q, own, cols:] = jnp.where(lanes < HALF, padded[q, own, cols:], tail)
-    lax.fori_loop(0, PLANES // 4, functools.partial(filter_columns, chosen=(0, blocks - 1)), 0)
+    for q in range(PLANES):
+        mask_and_shift(q)
+        filter_plane(q, range(1, blocks - 1))
 
     width = 2 * LANES
     partial[...] = jnp.zeros_like(partial)
@@ -233,11 +219,11 @@
         value = jnp.sum(value.reshape(-1, 8, width), axis=0)
         return value[:, :LANES] + value[:, LANES:]
 
-    def finish_tiles(p, tiles):
+    def finish_tiles(p, tiles, chunks):
         first = VARS * p
         for tile in tiles:
             own = pl.ds(tile * TILE, TILE)
-            for chunk in range(cols // width):
+            for chunk in chunks:
                 part = pl.ds(chunk * width, width)
                 terms = []
                 for k in range(KERNELS):
@@ -256,17 +242,46 @@
                     noise = nugget[v] * local
                     mixed = [term[v * TILE : (v + 1) * TILE] for term in terms]
                     total = (mixed[0] + mixed[1] + noise).astype(BF16)
-                    staged[first + v, own, part] = jnp.where(keep, total, jnp.zeros_like(total))
+                    out[first + v, own, part] = jnp.where(keep, total, jnp.zeros_like(total))
                     for k, term in enumerate(mixed + [noise]):
                         sums[k] = sums[k] + folded(term * local)
                 for k in range(KERNELS + 1):
                     partial[k, p] = partial[k, p] + sums[k]
 
-    def inner_tiles(p, carry):
-        finish_tiles(p, range(1, rows // TILE - 1))
+    def inner_tiles(p, carry, chunks):
+        finish_tiles(p, range(1, rows // TILE - 1), chunks)
         return carry
 
-    lax.fori_loop(0, PROBES, inner_tiles, 0)
+    chunks = cols // width
+    middle, ends = range(1, chunks - 1), (0, chunks - 1)
+    lax.fori_loop(0, PROBES, functools.partial(inner_tiles, chunks=middle), 0)
+
+    def unpack(west_halo, east_halo, a):
+        slot = lax.div(lane_of(west_halo.shape[0]), HALF)
+        both = jnp.where(slot == a, east_halo, west_halo)
+        turn = (1 - a) % GROUP * HALF
+        return pltpu.roll(both, turn, 1) if turn else both
+
+    for moves in edge_moves:
+        for move in moves[:2]:
+            move.wait_recv()
+
+    def outer_columns(g, carry):
+        for a in range(GROUP):
+            q = GROUP * g + a
+            halo = unpack(col_halo[0, g], col_halo[1, g], a)
+            padded[q, own, columns(0)] = jnp.where(lanes < HALF, halo, padded[q, own, columns(0)])
+            tail = jnp.where(lanes < 2 * HALF, halo, zero)
+            padded[q, own, columns(blocks)] = jnp.where(
+                lanes < HALF, padded[q, own, columns(blocks)], tail
+            )
+        for a in range(GROUP):
+            filter_plane(GROUP * g + a, (0, blocks - 1))
+        return carry
+
+    lax.fori_loop(0, PLANES // GROUP, outer_columns, 0)
+
+    lax.fori_loop(0, PROBES, functools.partial(inner_tiles, chunks=ends), 0)
 
     for g in range(PLANES // GROUP):
         for move in edge_moves[g][2:]:
@@ -319,17 +334,18 @@
     lax.fori_loop(0, PLANES // 4, filter_halo, 0)
 
     def outer_tiles(p, carry):
-        finish_tiles(p, (0, rows // TILE - 1))
-        some = pl.ds(VARS * p, VARS)
-        pltpu.make_async_copy(staged.at[some], out.at[some], store_sem.at[p]).start()
+        finish_tiles(p, (0, rows // TILE - 1), range(chunks))
         return carry
 
     lax.fori_loop(0, PROBES, outer_tiles, 0)
 
-    value = jnp.sum(partial[...].reshape(-1, 8, LANES), axis=1)
-    for number, (peers, slots) in enumerate(
-        ((band_peers, slots_a), (z_peers, slots_b), (x_peers, slots_c))
-    ):
+    count = (KERNELS + 1) * PROBES
+    value = jnp.sum(partial[...].reshape(count, 8, LANES), axis=1)
+    value = jnp.sum(value, axis=1, keepdims=True)
+    row = lax.broadcasted_iota(jnp.int32, (count, LANES), 0)
+    value = jnp.sum(jnp.where(lane_of(count) == row, value, 0.0), axis=0, keepdims=True)
+    share_moves = []
+    for number, (peers, slots) in enumerate(((near, slots_a), (far, slots_b))):
         if not peers:
             continue
         shares[number] = value
@@ -342,44 +358,41 @@
         ]
         for move in moves:
             move.start()
-        for d, move in enumerate(moves):
-            move.wait()
-        for d in range(len(peers)):
-            value = value + slots[d]
-    value = jnp.sum(value, axis=1, keepdims=True) * (1.0 / (bands * rows * cols))
+        for move in moves:
+            move.wait_recv()
+        value = value + jnp.sum(slots[: len(peers)], axis=0)
+        share_moves.append(moves)
+    value = jnp.broadcast_to(value * (1.0 / (bands * rows * cols)), (PROBES, LANES))
+    lane = lane_of(PROBES)
+    row = lax.broadcasted_iota(jnp.int32, (PROBES, LANES), 0)
     for k in range(KERNELS + 1):
-        quad[:, k : k + 1] = value[k * PROBES : (k + 1) * PROBES]
-
-    for moves in row_moves + edge_moves:
+        chosen = jnp.where(lane == k * PROBES + row, value, 0.0)
+        quad[:, k : k + 1] = jnp.sum(chosen, axis=1, keepdims=True)
+
+    for moves in row_moves + edge_moves + share_moves:
         for move in moves:
             move.wait_send()
-    for p in range(PROBES):
-        some = pl.ds(VARS * p, VARS)
-        pltpu.make_async_copy(staged.at[some], out.at[some], store_sem.at[p]).wait()
 
 
 def per_device(probes, filter_taps, mixing, nugget, land_span):
     rows, cols = probes.shape[2:]
-    bands = lax.axis_size("band")
     any_space = pl.BlockSpec(memory_space=pl.ANY)
     scalars = pl.BlockSpec(memory_space=pltpu.SMEM)
     vector = pl.BlockSpec(memory_space=pltpu.VMEM)
-    count = (KERNELS + 1) * PROBES
     dma = pltpu.SemaphoreType.DMA
     out, quadratic = pl.pallas_call(
         kernel,
         out_shape=(
-            jax.ShapeDtypeStruct((PLANES, rows, cols), BF16),
-            jax.ShapeDtypeStruct((PROBES, KERNELS + 1), F32),
+            pltpu.VMEM((PLANES, rows, cols), BF16),
+            pltpu.VMEM((PROBES, KERNELS + 1), F32),
         ),
         in_specs=[any_space, scalars, scalars, scalars, vector],
-        out_specs=(any_space, vector),
+        out_specs=(vector, vector),
         scratch_shapes=[
             pltpu.VMEM((PLANES, rows, cols), BF16),
             pltpu.VMEM((rows, cols), BF16),
             pltpu.VMEM((PLANES, rows + 2 * HALF, cols + LANES), BF16),
             pltpu.VMEM((KERNELS, PLANES, rows + 2 * HALF, cols), BF16),
-            pltpu.VMEM((PLANES, rows, cols), BF16),
             pltpu.VMEM((2 * LANES, KERNELS * LANES), BF16),
             pltpu.VMEM((KERNELS, VARS * TILE, VARS * WINDOW), BF16),
             pltpu.VMEM((2, PLANES // GROUP, rows, LANES), BF16),
@@ -387,10 +400,9 @@
             pltpu.VMEM((2, PLANES // GROUP, rows, LANES), BF16),
             pltpu.VMEM((2, 2, PLANES // GROUP, HALF, LANES), BF16),
             pltpu.VMEM((KERNELS + 1, PROBES, 8, LANES), F32),
-            pltpu.VMEM((3, count, LANES), F32),
-            pltpu.VMEM((max(bands - 1, 1), count, LANES), F32),
-            pltpu.VMEM((7, count, LANES), F32),
-            pltpu.VMEM((3, count, LANES), F32),
+            pltpu.VMEM((2, 1, LANES), F32),
+            pltpu.VMEM((15, 1, LANES), F32),
+            pltpu.VMEM((15, 1, LANES), F32),
             dma((PROBES,)),
             dma((2, PROBES)),
             dma((2, PROBES)),
@@ -398,9 +410,8 @@
             dma((2, PLANES // GROUP)),
             dma((2, 2, PLANES // GROUP)),
             dma((2, 2, PLANES // GROUP)),
-            dma((PROBES,)),
-            dma((3, 7)),
-            dma((3, 7)),
+            dma((2, 15)),
+            dma((2, 15)),
         ],
         compiler_params=pltpu.CompilerParams(
             collective_id=0, has_side_effects=True, vmem_limit_bytes=56 * 1024 * 1024

time: 42.1 us -> 36.3 us (0.86)
  Pallas kernels: 36 us -> 32.9 us
  local copies, waits for them, and re-layouts: 5.39 us -> 2.59 us
    pallas_call x1, Pallas kernels: 36 us -> 32.9 us  [per_device(): pl.pallas_call(kernel, out_shape=(pltpu.VMEM((PLANES, rows, cols), BF16),...]
    unnamed x4 -> x2, local copies, waits for them, and re-layouts: 5.39 us -> 2.59 us
where the time goes in v1:
time: 36.3 us; the launch traced here: 36.2 us
  Pallas kernels  32.9 us (91%)
  local copies, waits for them, and re-layouts  2.59 us (7%)
  between operations  0.64 us (2%)
    pallas_call x1, Pallas kernels, per_device(): pl.pallas_call(kernel, out_shape=(pltpu.VMEM((PLANES, rows, cols), BF16),...  32.9 us
    unnamed x2, local copies, waits for them, and re-layouts  2.59 us

profile of v1, /device:TPU:1, one launch (start us, length us, event | category | flops | bytes accessed | tf_op | source)
XLA Modules:
  0.0 36.2 jit_solution(3955528870687825806)
XLA Ops:
  0.6 32.9 %shard_map.68 = (bf16[16,128,1024]{2,1,0:T(8,128)(2,1)S(1)}, f32[4,3]{1,0:T(4,128)S(1)}) custom-call(bf16[16,128,1024]{2,1,0:T(8,128)(2,1)} %bitcast.4, f32[2,2,17]{2,1,0:T(2,128)} %taps.1, f32[2,4,4]{2,1,0:T(4,128)} %mixing.1, f32[4]{0:T(128)} %nugget.1, s32[2,1,128]{2,1,0:T(1,128)} %bitcast.5), custom_call_target="tpu_custom_call" | custom-call | tf_op jit(solution)/shard_map/pallas_call | solution.py:383
  33.6 2.0 %copy.9 = bf16[4,4,128,1024]{3,2,1,0:T(8,128)(2,1)} copy(bf16[4,4,128,1024]{3,2,1,0:T(8,128)(2,1)S(1)} %bitcast.3) | data formatting | bytes 8388608
  35.6 0.6 %copy.10 = f32[4,3]{1,0:T(4,128)} copy(f32[4,3]{1,0:T(4,128)S(1)} %get-tuple-element.7) | data formatting | bytes 96

commit v2 on v1

--- a/solution.py
+++ b/solution.py
@@ -32,10 +32,10 @@
 
 
 def kernel(
-    probes, taps, mixing, nugget, span, out, quad,
-    held, land, padded, across, column_filter, row_filter, edges,
+    probes, taps_in, mixing_in, nugget_in, span_in, out, quad,
+    taps, mixing, nugget, span, held, land, padded, across, column_filter, row_filter, edges,
     row_halo, col_halo, corner_halo, partial, shares, slots_a, slots_b,
-    load_sem, row_send, row_recv, col_send, col_recv, corner_send, corner_recv,
+    param_sem, load_sem, row_send, row_recv, col_send, col_recv, corner_send, corner_recv,
     share_send, share_recv,
 ):
     rows, cols = held.shape[1:]
@@ -52,29 +52,59 @@
     cores = 2
     strips = bands // cores
     at_y, core = lax.div(band, cores), lax.rem(band, cores)
+
+    def hops(step, size):
+        return min(step, size - step)
+
+    def far_first(steps, length):
+        return sorted(steps, key=length, reverse=True)
+
     near = [
-        (base_z + lax.rem(at_z + d // cores, across_z), at_y * cores + lax.rem(core + d, cores))
-        for d in range(1, across_z * cores)
+        (base_z + lax.rem(at_z + z, across_z), at_y * cores + lax.rem(core + c, cores))
+        for z, c in far_first(
+            [divmod(d, cores) for d in range(1, across_z * cores)],
+            lambda step: hops(step[0], across_z) * cores + step[1],
+        )
     ]
     far = [
-        (lax.rem(region + d // strips * across_z, regions), lax.rem(band + d % strips * cores, bands))
-        for d in range(1, across_x * strips)
+        (lax.rem(region + x * across_z, regions), lax.rem(band + y * cores, bands))
+        for x, y in far_first(
+            [divmod(d, strips) for d in range(1, across_x * strips)],
+            lambda step: hops(step[0], across_x) + hops(step[1], strips),
+        )
     ]
     corners = [(east, south), (east, north), (west, south), (west, north)]
     greeted = near + far + [(region, south), (region, north), (east, band), (west, band)] + corners
 
+    params = [
+        pltpu.make_async_copy(source, target, param_sem.at[number])
+        for number, (source, target) in enumerate(
+            ((span_in, span), (taps_in, taps), (mixing_in, mixing), (nugget_in, nugget))
+        )
+    ]
+    params[0].start()
+    high, low = pl.ds(0, HALF), pl.ds(rows - HALF, HALF)
+    middle_rows = pl.ds(HALF, rows - 2 * HALF)
+    left, right = pl.ds(0, LANES), pl.ds(cols - LANES, LANES)
+    whole, inside = pl.ds(0, cols), pl.ds(LANES, cols - 2 * LANES)
+    every = pl.ds(0, PLANES)
+    regions_of_load = [
+        (every, high, whole), (every, low, whole),
+        (every, middle_rows, left), (every, middle_rows, right),
+    ] + [(pl.ds(VARS * p, VARS), middle_rows, inside) for p in range(PROBES)]
     loads = [
-        pltpu.make_async_copy(
-            probes.at[pl.ds(VARS * p, VARS)], held.at[pl.ds(VARS * p, VARS)], load_sem.at[p]
-        )
-        for p in range(PROBES)
+        pltpu.make_async_copy(probes.at[part], held.at[part], load_sem.at[number])
+        for number, part in enumerate(regions_of_load)
     ]
     for load in loads:
         load.start()
+    for param in params[1:]:
+        param.start()
     barrier = pltpu.get_barrier_semaphore()
     for peer in greeted:
         pl.semaphore_signal(barrier, inc=1, device_id=peer, device_id_type=MESH)
 
+    params[0].wait()
     def by_row(entry):
         line = span[entry].astype(F32)
         return jnp.transpose(jnp.broadcast_to(line, (LANES, rows)))
@@ -84,25 +114,6 @@
         column = (lane_of(rows) + block * LANES).astype(F32)
         inside = (column >= lower) & (column < upper)
         land[:, block * LANES : (block + 1) * LANES] = jnp.where(inside, 1.0, 0.0).astype(BF16)
-
-    def rounded(k, axis):
-        return lambda step: jnp.full((1, 1), taps[k, axis, step], F32).astype(BF16).astype(F32)
-
-    shape = (2 * LANES, LANES)
-    offset = lax.broadcasted_iota(jnp.int32, shape, 0) - lax.broadcasted_iota(jnp.int32, shape, 1)
-    for k in range(KERNELS):
-        column_filter[:, k * LANES : (k + 1) * LANES] = toeplitz(offset, rounded(k, 0)).astype(BF16)
-    shape = (TILE, LANES)
-    lane = lax.broadcasted_iota(jnp.int32, shape, 1)
-    offset = lax.rem(lane, WINDOW) - lax.broadcasted_iota(jnp.int32, shape, 0)
-    for k in range(KERNELS):
-        pattern = toeplitz(offset, rounded(k, 1))
-        for v in range(VARS):
-            for w in range(0, VARS, 2):
-                gains = jnp.where(lane < WINDOW, mixing[k, v, w], mixing[k, v, w + 1])
-                row_filter[k, v * TILE : (v + 1) * TILE, w * WINDOW : (w + 2) * WINDOW] = (
-                    gains * pattern
-                ).astype(BF16)
 
     lanes = lane_of(rows)
     zero = jnp.zeros((rows, LANES), BF16)
@@ -191,9 +202,10 @@
                 across[k, q, own, columns(j)] = both[:, columns(k)]
 
     row_moves, edge_moves = [], []
+    for load in loads[:4]:
+        load.wait()
     packed = [zero, zero]
     for p in range(PROBES):
-        loads[p].wait()
         for q in range(VARS * p, VARS * (p + 1)):
             packed = mask_borders(q, q % GROUP, packed)
         if p == 0:
@@ -208,7 +220,30 @@
             edge_moves.append(edge_copies(g))
             for move in edge_moves[-1]:
                 move.start()
+    for param in params[1:]:
+        param.wait()
+    def rounded(k, axis):
+        return lambda step: jnp.full((1, 1), taps[k, axis, step], F32).astype(BF16).astype(F32)
+
+    shape = (2 * LANES, LANES)
+    offset = lax.broadcasted_iota(jnp.int32, shape, 0) - lax.broadcasted_iota(jnp.int32, shape, 1)
+    for k in range(KERNELS):
+        column_filter[:, k * LANES : (k + 1) * LANES] = toeplitz(offset, rounded(k, 0)).astype(BF16)
+    shape = (TILE, LANES)
+    lane = lax.broadcasted_iota(jnp.int32, shape, 1)
+    offset = lax.rem(lane, WINDOW) - lax.broadcasted_iota(jnp.int32, shape, 0)
+    for k in range(KERNELS):
+        pattern = toeplitz(offset, rounded(k, 1))
+        for v in range(VARS):
+            for w in range(0, VARS, 2):
+                gains = jnp.where(lane < WINDOW, mixing[k, v, w], mixing[k, v, w + 1])
+                row_filter[k, v * TILE : (v + 1) * TILE, w * WINDOW : (w + 2) * WINDOW] = (
+                    gains * pattern
+                ).astype(BF16)
+
     for q in range(PLANES):
+        if q % VARS == 0:
+            loads[4 + q // VARS].wait()
         mask_and_shift(q)
         filter_plane(q, range(1, blocks - 1))
 
@@ -248,13 +283,17 @@
                 for k in range(KERNELS + 1):
                     partial[k, p] = partial[k, p] + sums[k]
 
-    def inner_tiles(p, carry, chunks):
-        finish_tiles(p, range(1, rows // TILE - 1), chunks)
+    pair = GROUP // VARS
+    inner, outer = range(1, rows // TILE - 1), (0, rows // TILE - 1)
+
+    def middle_tiles(g, carry):
+        for p in range(pair):
+            finish_tiles(pair * g + p, inner, middle)
         return carry
 
     chunks = cols // width
     middle, ends = range(1, chunks - 1), (0, chunks - 1)
-    lax.fori_loop(0, PROBES, functools.partial(inner_tiles, chunks=middle), 0)
+    lax.fori_loop(0, PLANES // GROUP, middle_tiles, 0)
 
     def unpack(west_halo, east_halo, a):
         slot = lax.div(lane_of(west_halo.shape[0]), HALF)
@@ -277,67 +316,58 @@
             )
         for a in range(GROUP):
             filter_plane(GROUP * g + a, (0, blocks - 1))
+        for p in range(pair):
+            finish_tiles(pair * g + p, inner, ends)
         return carry
 
     lax.fori_loop(0, PLANES // GROUP, outer_columns, 0)
 
-    lax.fori_loop(0, PROBES, functools.partial(inner_tiles, chunks=ends), 0)
-
-    for g in range(PLANES // GROUP):
-        for move in edge_moves[g][2:]:
-            move.wait_recv()
-    for p in range(PROBES):
-        for move in row_moves[p]:
-            move.wait_recv()
 
     beyond = [(band > 0).astype(F32).astype(BF16), (band < bands - 1).astype(F32).astype(BF16)]
     short = lane_of(HALF)
     none = jnp.zeros((HALF, LANES), BF16)
-    def halo_rows(g, carry):
-        for a in range(GROUP):
-            q = GROUP * g + a
-            for end, place in ((0, 0), (1, HALF + rows)):
-                halo = unpack(corner_halo[0, end, g], corner_halo[1, end, g], a)
-
-                def store(j, value):
-                    padded[q, place : place + HALF, j * LANES : (j + 1) * LANES] = (
-                        value * beyond[end]
-                    )
-
-                last = shifted(
-                    lambda j: row_halo[end, q, :, j * LANES : (j + 1) * LANES], halo, store
-                )
-                tail = jnp.where(short < 2 * HALF, halo, none)
-                store(blocks, jnp.where(short < HALF, last, tail))
-        return carry
-
-    lax.fori_loop(0, PLANES // GROUP, halo_rows, 0)
-
-    def filter_halo(number, carry):
-        ends = (0, HALF + rows)
+    def halo_plane(q, g, a):
+        for end, place in ((0, 0), (1, HALF + rows)):
+            halo = unpack(corner_halo[0, end, g], corner_halo[1, end, g], a)
+
+            def store(j, value):
+                padded[q, place : place + HALF, columns(j)] = value * beyond[end]
+
+            last = shifted(lambda j: row_halo[end, q, :, columns(j)], halo, store)
+            tail = jnp.where(short < 2 * HALF, halo, none)
+            store(blocks, jnp.where(short < HALF, last, tail))
+
+    def filter_halo(number):
+        places = (0, HALF + rows)
         for j in range(blocks):
-            part = slice(j * LANES, (j + 2) * LANES)
             window = jnp.concatenate(
-                [padded[4 * number + u, at : at + HALF, part] for u in range(4) for at in ends],
+                [
+                    padded[VARS * number + v, at : at + HALF, columns(j, 2)]
+                    for v in range(VARS)
+                    for at in places
+                ],
                 axis=0,
             )
             both = jnp.dot(window, column_filter[...], preferred_element_type=F32).astype(BF16)
-            for u in range(4):
-                for end, at in enumerate(ends):
-                    start = (2 * u + end) * HALF
+            for v in range(VARS):
+                for end, at in enumerate(places):
+                    start = (2 * v + end) * HALF
                     for k in range(KERNELS):
-                        across[
-                            k, 4 * number + u, at : at + HALF, j * LANES : (j + 1) * LANES
-                        ] = both[start : start + HALF, k * LANES : (k + 1) * LANES]
-        return carry
-
-    lax.fori_loop(0, PLANES // 4, filter_halo, 0)
-
-    def outer_tiles(p, carry):
-        finish_tiles(p, (0, rows // TILE - 1), range(chunks))
-        return carry
-
-    lax.fori_loop(0, PROBES, outer_tiles, 0)
+                        across[k, VARS * number + v, at : at + HALF, columns(j)] = both[
+                            start : start + HALF, columns(k)
+                        ]
+
+    for p in range(PROBES):
+        if p * VARS % GROUP == 0:
+            for move in edge_moves[p * VARS // GROUP][2:]:
+                move.wait_recv()
+        for move in row_moves[p]:
+            move.wait_recv()
+        for q in range(VARS * p, VARS * (p + 1)):
+            halo_plane(q, q // GROUP, q % GROUP)
+        filter_halo(p)
+        finish_tiles(p, outer, range(chunks))
+
 
     count = (KERNELS + 1) * PROBES
     value = jnp.sum(partial[...].reshape(count, 8, LANES), axis=1)
@@ -377,7 +407,6 @@
 def per_device(probes, filter_taps, mixing, nugget, land_span):
     rows, cols = probes.shape[2:]
     any_space = pl.BlockSpec(memory_space=pl.ANY)
-    scalars = pl.BlockSpec(memory_space=pltpu.SMEM)
     vector = pl.BlockSpec(memory_space=pltpu.VMEM)
     dma = pltpu.SemaphoreType.DMA
     out, quadratic = pl.pallas_call(
@@ -386,9 +415,13 @@
             pltpu.VMEM((PLANES, rows, cols), BF16),
             pltpu.VMEM((PROBES, KERNELS + 1), F32),
         ),
-        in_specs=[any_space, scalars, scalars, scalars, vector],
+        in_specs=[any_space] * 5,
         out_specs=(vector, vector),
         scratch_shapes=[
+            pltpu.SMEM(filter_taps.shape, F32),
+            pltpu.SMEM(mixing.shape, F32),
+            pltpu.SMEM(nugget.shape, F32),
+            pltpu.VMEM((2, 1, rows), jnp.int32),
             pltpu.VMEM((PLANES, rows, cols), BF16),
             pltpu.VMEM((rows, cols), BF16),
             pltpu.VMEM((PLANES, rows + 2 * HALF, cols + LANES), BF16),
@@ -403,7 +436,8 @@
             pltpu.VMEM((2, 1, LANES), F32),
             pltpu.VMEM((15, 1, LANES), F32),
             pltpu.VMEM((15, 1, LANES), F32),
-            dma((PROBES,)),
+            dma((4,)),
+            dma((4 + PROBES,)),
             dma((2, PROBES)),
             dma((2, PROBES)),
             dma((2, PLANES // GROUP)),

time: 36.3 us -> 33.6 us (0.926)
  Pallas kernels: 32.9 us -> 30.3 us
    pallas_call x1, Pallas kernels: 32.9 us -> 30.3 us  [per_device(): pl.pallas_call(kernel, out_shape=(pltpu.VMEM((PLANES, rows, cols), BF16),...]
where the time goes in v2:
time: 33.6 us; the launch traced here: 33.5 us
  Pallas kernels  30.3 us (90%)
  local copies, waits for them, and re-layouts  2.59 us (8%)
  between operations  0.64 us (2%)
    pallas_call x1, Pallas kernels, per_device(): pl.pallas_call(kernel, out_shape=(pltpu.VMEM((PLANES, rows, cols), BF16),...  30.3 us
    unnamed x2, local copies, waits for them, and re-layouts  2.59 us

profile of v2, /device:TPU:1, one launch (start us, length us, event | category | flops | bytes accessed | tf_op | source)
XLA Modules:
  0.0 33.5 jit_solution(14719395690880125841)
XLA Ops:
  0.6 30.3 %shard_map.68 = (bf16[16,128,1024]{2,1,0:T(8,128)(2,1)S(1)}, f32[4,3]{1,0:T(4,128)S(1)}) custom-call(bf16[16,128,1024]{2,1,0:T(8,128)(2,1)} %bitcast.4, f32[2,2,17]{2,1,0:T(2,128)} %taps_in.1, f32[2,4,4]{2,1,0:T(4,128)} %mixing_in.1, f32[4]{0:T(128)} %nugget_in.1, s32[2,1,128]{2,1,0:T(1,128)} %bitcast.5), custom_call_target="tpu_custom_call" | custom-call | tf_op jit(solution)/shard_map/pallas_call | solution.py:412
  30.9 2.0 %copy.9 = bf16[4,4,128,1024]{3,2,1,0:T(8,128)(2,1)} copy(bf16[4,4,128,1024]{3,2,1,0:T(8,128)(2,1)S(1)} %bitcast.3) | data formatting | bytes 8388608
  32.9 0.6 %copy.10 = f32[4,3]{1,0:T(4,128)} copy(f32[4,3]{1,0:T(4,128)S(1)} %get-tuple-element.7) | data formatting | bytes 96

commit v3 on v2

--- a/solution.py
+++ b/solution.py
@@ -167,9 +167,11 @@
                 )
         return copies
 
-    def mask_borders(q, a, packed):
+    def mask_rows(q):
         for place in (slice(0, HALF), slice(rows - HALF, rows)):
             held[q, place] = held[q, place] * land[place]
+
+    def pack_edges(q, a, packed):
         both = jnp.where(lanes < HALF, held[q, :, columns(0)], held[q, :, columns(blocks - 1)])
         both = both * jnp.where(lanes < HALF, land[:, columns(0)], land[:, columns(blocks - 1)])
         both = pltpu.roll(both, a * HALF, 1) if a else both
@@ -202,17 +204,22 @@
                 across[k, q, own, columns(j)] = both[:, columns(k)]
 
     row_moves, edge_moves = [], []
-    for load in loads[:4]:
+    for load in loads[:2]:
         load.wait()
-    packed = [zero, zero]
     for p in range(PROBES):
         for q in range(VARS * p, VARS * (p + 1)):
-            packed = mask_borders(q, q % GROUP, packed)
+            mask_rows(q)
         if p == 0:
             pl.semaphore_wait(barrier, len(greeted))
         row_moves.append(row_copies(p))
         for move in row_moves[-1]:
             move.start()
+    for load in loads[2:4]:
+        load.wait()
+    packed = [zero, zero]
+    for p in range(PROBES):
+        for q in range(VARS * p, VARS * (p + 1)):
+            packed = pack_edges(q, q % GROUP, packed)
         if (p + 1) * VARS % GROUP == 0:
             g = p * VARS // GROUP
             edges[0, g], edges[1, g] = packed

time: 33.6 us -> 33.7 us (level)
  no operation moved by 1% of the time
where the time goes in v3:
time: 33.7 us; the launch traced here: 33.6 us
  Pallas kernels  30.4 us (90%)
  local copies, waits for them, and re-layouts  2.59 us (8%)
  between operations  0.64 us (2%)
    pallas_call x1, Pallas kernels, per_device(): pl.pallas_call(kernel, out_shape=(pltpu.VMEM((PLANES, rows, cols), BF16),...  30.4 us
    unnamed x2, local copies, waits for them, and re-layouts  2.59 us

profile of v3, /device:TPU:1, one launch (start us, length us, event | category | flops | bytes accessed | tf_op | source)
XLA Modules:
  0.0 33.6 jit_solution(12792006878176838582)
XLA Ops:
  0.6 30.4 %shard_map.68 = (bf16[16,128,1024]{2,1,0:T(8,128)(2,1)S(1)}, f32[4,3]{1,0:T(4,128)S(1)}) custom-call(bf16[16,128,1024]{2,1,0:T(8,128)(2,1)} %bitcast.4, f32[2,2,17]{2,1,0:T(2,128)} %taps_in.1, f32[2,4,4]{2,1,0:T(4,128)} %mixing_in.1, f32[4]{0:T(128)} %nugget_in.1, s32[2,1,128]{2,1,0:T(1,128)} %bitcast.5), custom_call_target="tpu_custom_call" | custom-call | tf_op jit(solution)/shard_map/pallas_call | solution.py:419
  31.0 2.0 %copy.9 = bf16[4,4,128,1024]{3,2,1,0:T(8,128)(2,1)} copy(bf16[4,4,128,1024]{3,2,1,0:T(8,128)(2,1)S(1)} %bitcast.3) | data formatting | bytes 8388608
  33.0 0.6 %copy.10 = f32[4,3]{1,0:T(4,128)} copy(f32[4,3]{1,0:T(4,128)S(1)} %get-tuple-element.7) | data formatting | bytes 96
